TPU v7x, 256 devices: a whole 4x4x8 slice. The times are simulated.
256 devices in a mesh: lat: 16 (over z_lo, y, core), lev: 4 (over x), ocn: 4 (over z_hi).
Axes of the slice: x: 4, y: 4, z: 8 (z_hi: 4, z_lo: 2; z = z_hi * 2 + z_lo), core: 2. Of those that a mesh axis runs over, the one named last changes fastest.
Arguments:
- atmos_fields: bfloat16 [2, 24, 2560, 5632], P(None, 'lev', ('lat', 'ocn')), may hold values from -6 to 6
- lat_points: int32 [2560], P(('lat', 'ocn')), may hold values from 20 to 5632, as said below
- wave_order: int32 [256], replicated, may hold values from 0 to 255, each once
- legendre: bfloat16 [256, 2560, 1536], P(('lat', 'ocn'), None, 'lev'), may hold values from -0.125 to 0.125
- column_weight: bfloat16 [2, 24], P(None, 'lev'), may hold values from -1.25 to 1.25
- block_remap: int32 [2560, 44], P(('lat', 'ocn'), 'lev'), may hold values from 0 to 17407, as said below
- ocean_temp: float32 [1024, 2176], P(('lat', 'ocn')), may hold values from -6 to 6
- ocean_salt: float32 [1024, 2176], P(('lat', 'ocn')), may hold values from -6 to 6
- sea_mask: int32 [1024, 17], P(('lat', 'ocn')), may hold values 0 or 1
Outputs:
- spectra: float32 [256, 96, 1536], P(('lat', 'ocn'), None, 'lev')
- temp_next: float32 [1024, 2176], P(('lat', 'ocn'))
- salt_next: float32 [1024, 2176], P(('lat', 'ocn'))
- surface_temp: float32 [2560, 5632], P(('lat', 'ocn'), 'lev')
Inputs may be any that keep to these rules, and one draw needn't show every extreme that they name: `lat_points`: a multiple of 4 for every latitude row. `wave_order`: each wavenumber appears once. `block_remap`: the blocks of latitude band g (rows g * 40 onward) name tiles of ocean sections g - 1, g or g + 1 only; section g holds tiles g * 16 * 17 onward, in row order.
All inputs are finite; a program needn't handle non-finite values. No bound on the sum of `sea_mask` on one device may be relied on, other than what follows from the above.
Results may differ from a plain program's by a relative error of at most 0.0037.
Values may be sent and summed in bfloat16 or wider, within the bound.
A program may use at most 128 MiB of HBM per device.

v0:
```python
import math
import jax
import jax.numpy as jnp
from jax import lax
from jax.sharding import PartitionSpec as P

FIELDS = 2
BLOCK = 128
FULL_TURN = 2.0 * math.pi
DIFFUSION = 0.2
COUPLING = 0.5


def with_halo(cells, sides, width):
    for axis, dim in sides:
        count = lax.axis_size(axis)
        ends = count - 1
        head = lax.slice_in_dim(cells, 0, width, axis=dim)
        tail = lax.slice_in_dim(cells, cells.shape[dim] - width, cells.shape[dim], axis=dim)
        cells = jnp.concatenate(
            [
                lax.ppermute(tail, axis, [(i, (i + 1) % count) for i in range(ends)]),
                cells,
                lax.ppermute(head, axis, [((i + 1) % count, i) for i in range(ends)]),
            ],
            axis=dim,
        )
    return cells


def fourier_table(wave_order, length):
    points = jnp.arange(length, dtype=jnp.int32)
    phase = wave_order[None, :] * points[:, None] % length
    angle = phase.astype(jnp.float32) * (FULL_TURN / length)
    table = jnp.concatenate([jnp.cos(angle), -jnp.sin(angle)], axis=1).astype(jnp.bfloat16)
    return (table, points)


def body(
    atmos_fields,
    lat_points,
    wave_order,
    legendre,
    column_weight,
    block_remap,
    ocean_temp,
    ocean_salt,
    sea_mask,
):
    nfields, lev_dev, lat_band, lon_count = atmos_fields.shape
    wave_count = wave_order.shape[0]
    table, points = fourier_table(wave_order, lon_count)
    point_mask = points[None, :] < lat_points[:, None]
    masked = jnp.where(point_mask[None, None], atmos_fields, jnp.zeros((), jnp.bfloat16))
    inverse_root = 1.0 / jnp.sqrt(lat_points.astype(jnp.float32))
    weights = jnp.where(
        2 * wave_order[None, :] < lat_points[:, None],
        inverse_root[:, None],
        jnp.zeros((), jnp.float32),
    )
    field_count = masked.shape[0]
    raw_sums = jnp.dot(masked.reshape(-1, lon_count), table, preferred_element_type=jnp.float32)
    raw_sums = raw_sums.reshape(field_count, lev_dev, lat_band, 2, wave_count)
    coeffs = (raw_sums * weights[None, None, :, None, :]).astype(jnp.bfloat16)
    regrouped = lax.all_to_all(
        coeffs.transpose(4, 1, 0, 3, 2).reshape(wave_count, lev_dev * field_count * 2, lat_band),
        ("lat", "ocn"),
        split_axis=0,
        concat_axis=2,
        tiled=True,
    )
    spectra = jnp.einsum(
        "srj,sjd->srd",
        lax.all_gather(regrouped, "lev", axis=1, tiled=True),
        legendre,
        preferred_element_type=jnp.float32,
    )
    ocean_rows, ocean_cols = ocean_temp.shape
    tile_count = ocean_rows * ocean_cols // BLOCK
    band_index = lax.axis_index(("lat", "ocn"))
    targets = block_remap.reshape(-1)
    local_slot = (targets // tile_count - band_index + 1) * tile_count + targets % tile_count
    partial_sum = jnp.einsum(
        "ql,qljk->qjk", column_weight, masked, preferred_element_type=jnp.float32
    )
    quarter = lon_count // lax.axis_size("lev")
    totals = lax.psum(partial_sum, "lev")
    own_flux = lax.dynamic_slice_in_dim(totals, lax.axis_index("lev") * quarter, quarter, 2)
    block_rows = (
        own_flux.reshape(FIELDS, lat_band, quarter // BLOCK, BLOCK)
        .transpose(1, 2, 0, 3)
        .reshape(-1, FIELDS * BLOCK)
    )
    outgoing = jax.ops.segment_sum(block_rows, local_slot, num_segments=3 * tile_count)
    widened = with_halo(outgoing, ((("lat", "ocn"), 0),), tile_count)
    arrived = (
        widened[:tile_count] + widened[2 * tile_count : 3 * tile_count] + widened[4 * tile_count :]
    )
    tile_sums = lax.psum(arrived, "lev")
    forcing = (
        tile_sums.reshape(ocean_rows, ocean_cols // BLOCK, FIELDS, BLOCK)
        .transpose(2, 0, 1, 3)
        .reshape(FIELDS, ocean_rows, ocean_cols)
    )
    sea_cells = (
        jnp.broadcast_to(sea_mask[:, :, None], (ocean_rows, ocean_cols // BLOCK, BLOCK))
        .reshape(ocean_rows, ocean_cols)
        .astype(jnp.float32)
    )
    ocean_state = jnp.stack([ocean_temp, ocean_salt])
    padded = with_halo(ocean_state, ((("lat", "ocn"), 1),), 1)
    laplace = (
        padded[:, 2:]
        + padded[:, :-2]
        + jnp.roll(ocean_state, 1, 2)
        + jnp.roll(ocean_state, -1, 2)
        - 4.0 * ocean_state
    )
    updated = ocean_state + DIFFUSION * laplace + COUPLING * sea_cells[None] * forcing
    temp_next = updated[0]
    salt_next = updated[1]
    returned = with_halo(temp_next, ((("lat", "ocn"), 0),), ocean_rows)
    tiles_near = returned.reshape(3 * tile_count, BLOCK)
    surface = jnp.take(tiles_near, local_slot, axis=0).reshape(lat_band, quarter)
    own_points = lax.axis_index("lev") * quarter + jnp.arange(quarter, dtype=jnp.int32)
    surface_temp = jnp.where(
        own_points[None, :] < lat_points[:, None], surface, jnp.zeros((), jnp.float32)
    )
    return (spectra, temp_next, salt_next, surface_temp)


def solution(mesh):
    placed = (
        P(None, "lev", ("lat", "ocn"), None),
        P(("lat", "ocn")),
        P(),
        P(("lat", "ocn"), None, "lev"),
        P(None, "lev"),
        P(("lat", "ocn"), "lev"),
        P(("lat", "ocn"), None),
        P(("lat", "ocn"), None),
        P(("lat", "ocn"), None),
    )
    return jax.shard_map(
        body,
        mesh=mesh,
        in_specs=placed,
        out_specs=(
            P(("lat", "ocn"), None, "lev"),
            P(("lat", "ocn"), None),
            P(("lat", "ocn"), None),
            P(("lat", "ocn"), "lev"),
        ),
        check_vma=False,
    )
```

profile of v0, /device:TPU:1, one launch (start us, length us, event | category | flops | bytes accessed | tf_op | source)
XLA Modules:
  0.0 199.3 jit_solution(3094316823144433169)
XLA Ops:
  7.2 0.0 copy-start
  7.2 0.0 all-reduce.3.cloned.1.call-start
  7.2 0.8 iota_compare_fusion
  8.1 3.6 %broadcast_select_fusion = bf16[2,6,40,5632]{3,2,1,0:T(8,128)(2,1)S(1)} fusion(bf16[2,6,40,5632]{3,2,1,0:T(8,128)(2,1)} %param.9, pred[40,5632]{1,0:T(8,128)(4,1)S(1)} %iota_compare_fusion), kind=kLoop, calls=%fused_computation.16 | loop fusion | flops 2703360 | bytes 11038720 | tf_op jit(solution)/shard_map/jit(_where)/select_n | solution.py:54
  11.7 0.0 copy-start.7
  11.7 0.0 copy-start.8
  11.7 2.4 %fusion = f32[2,1,40,5632]{3,1,2,0:T(1,128)S(1)} fusion(bf16[2,6,40,5632]{3,2,1,0:T(8,128)(2,1)S(1)} %broadcast_select_fusion, bf16[2,6,1,1]{1,0,2,3:T(2,128)(2,1)S(1)} %bitcast.59), kind=kOutput, calls=%fused_computation.3 | convolution fusion | flops 5406720 | bytes 7208984 | tf_op jit(solution)/shard_map/ql,qljk->qjk/dot_general | solution.py:83
  14.2 1.4 copy.59
  15.5 0.0 all-reduce.3.cloned.1.call-update
  15.6 0.0 slice-start
  15.6 25.0 %cosine_convert_fusion = (bf16[5632,256]{0,1:T(8,128)(2,1)S(1)}, bf16[5632,256]{0,1:T(8,128)(2,1)S(1)}) fusion(s32[256]{0:T(256)S(1)} %copy-done.8), kind=kLoop, calls=%fused_computation.9 | loop fusion | flops 17301504 | bytes 5768192 | tf_op jit(solution)/shard_map/convert
  40.6 0.0 slice-start.1
  40.7 2.9 %pad_maximum_fusion = bf16[5632,512]{0,1:T(8,128)(2,1)} fusion(bf16[5632,256]{0,1:T(8,128)(2,1)S(1)} %get-tuple-element.21, bf16[5632,256]{0,1:T(8,128)(2,1)S(1)} %get-tuple-element.20), kind=kLoop, calls=%fused_computation.7 | loop fusion | flops 11534336 | bytes 11534336 | tf_op jit(solution)/shard_map/concatenate | solution.py:35
  43.5 0.1 compare_select_fusion
  43.6 5.7 %fusion.15 = bf16[256,6,2,2,40]{0,4,3,1,2:T(8,128)(2,1)S(1)} fusion(bf16[2,256,5632,1,1]{2,1,0,4,3:T(8,128)(2,1)} %bitcast.64, bf16[2,6,40,5632]{3,2,1,0:T(8,128)(2,1)S(1)} %bitcast.61, f32[256,40]{0,1:T(8,128)S(1)} %compare_select_fusion), kind=kOutput, calls=%fused_computation.20 | convolution fusion | flops 2768732160 | bytes 11706368 | tf_op jit(solution)/shard_map/dot_general | solution.py:62
  49.3 0.0 copy-start.5
  49.4 1.0 copy.32
  50.3 3.4 %reshape.235 = bf16[64,2,1920]{2,1,0:T(2,128)(2,1)} reshape(bf16[256,24,40]{2,1,0:T(8,128)(2,1)S(1)} %copy.32) | data formatting | bytes 983040
  53.7 13.3 %all-to-all-start = ((bf16[64,2,1920]{2,1,0:T(2,128)(2,1)}), bf16[64,2,1920]{2,1,0:T(2,128)(2,1)S(1)}, u32[]{:S(2)}, u32[]{:S(2)}) async-start(bf16[64,2,1920]{2,1,0:T(2,128)(2,1)} %reshape.235), calls=%async_computation | async-start | bytes 983040 | tf_op jit(solution)/shard_map/all_to_all | solution.py:65
  67.1 0.0 all-reduce.5.cloned.1.call-start
  67.2 0.1 copy.35
  67.2 0.1 rem.47
  67.4 0.1 copy.36
  67.5 0.1 div.26
  67.6 0.1 copy.34
  67.7 0.1 ne.88
  67.9 10.6 %all-reduce.3.cloned.1.call-done = f32[2,40,5632]{2,1,0:T(8,128)} async-done(((f32[2,40,5632]{2,1,0:T(8,128)}), f32[2,40,5632]{2,1,0:T(8,128)}) %all-reduce.3.cloned.1.call-update) | async-done | bytes 1802256 | tf_op jit(solution)/shard_map/psum | solution.py:87
  78.5 1.0 constant_dynamic-slice_fusion
  79.6 0.1 reshape.208
  79.6 0.3 copy.37
  80.0 3.1 %scatter_custom_fusion = f32[816,256]{1,0:T(8,128)S(1)} fusion(s32[440]{0:T(512)S(1)} %bitcast.81, f32[55,8,2,128]{3,2,1,0:T(2,128)S(1)} %bitcast.75, f32[]{:T(128)} %constant.40.clone.1), kind=kCustom, calls=%fused_computation.35 | custom fusion | flops 112640 | bytes 1286148 | tf_op jit(solution)/shard_map/scatter-add | solution.py:94
  83.2 6.3 %collective-permute-start.3 = (f32[272,256]{1,0:T(8,128)S(1)}, f32[272,256]{1,0:T(8,128)S(1)}, u32[]{:S(2)}, u32[]{:S(2)}) collective-permute-start(f32[272,256]{1,0:T(8,128)S(1)} %get-tuple-element.9), channel_id=1, source_target_pairs={{1,0},{2,1},{3,2},{16,3},{17,16},{18,17},{19,18},{32,19},{33,32},{... | collective-permute-start | bytes 835592 | tf_op jit(solution)/shard_map/ppermute | solution.py:24
  89.5 1.9 collective-permute-start.2
  91.4 8.1 %collective-permute-done.3 = f32[272,256]{1,0:T(8,128)S(1)} collective-permute-done((f32[272,256]{1,0:T(8,128)S(1)}, f32[272,256]{1,0:T(8,128)S(1)}, u32[]{:S(2)}, u32[]{:S(2)}) %collective-permute-start.3) | collective-permute-done | bytes 278560 | tf_op jit(solution)/shard_map/ppermute | solution.py:24
  99.6 8.0 %collective-permute-done.2 = f32[272,256]{1,0:T(8,128)S(1)} collective-permute-done((f32[272,256]{1,0:T(8,128)S(1)}, f32[272,256]{1,0:T(8,128)S(1)}, u32[]{:S(2)}, u32[]{:S(2)}) %collective-permute-start.2) | collective-permute-done | bytes 278560 | tf_op jit(solution)/shard_map/ppermute | solution.py:22
  107.6 0.1 fusion.24
  107.6 0.0 copy-start.6
  107.7 0.1 reshape.210
  107.9 0.8 reshape.211
  108.6 0.0 all-reduce.5.cloned.1.call-update
  108.6 0.0 all-gather.2.cloned.1.call-start
  108.7 1.9 collective-permute-start.1
  110.7 5.8 %collective-permute-start = (f32[2,1,2176]{2,1,0:T(1,128)S(1)}, f32[2,1,2176]{2,1,0:T(1,128)S(1)}, u32[]{:S(2)}, u32[]{:S(2)}) collective-permute-start(f32[2,1,2176]{2,1,0:T(1,128)S(1)} %get-tuple-element.16), channel_id=1, source_target_pairs={{1,0},{2,1},{3,2},{16,3},{17,16},{18,17},{19,18},{32,19},{33,32},{... | collective-permute-start | bytes 52232 | tf_op jit(solution)/shard_map/ppermute | solution.py:24
  116.4 2.5 %reshape.236 = bf16[256,24,40]{2,1,0:T(8,128)(2,1)S(1)} reshape(bf16[64,2,1920]{2,1,0:T(2,128)(2,1)S(1)} %all-to-all-done) | data formatting | bytes 983040
  119.0 0.6 copy.33
  119.6 3.9 %all_to_all.16 = bf16[4,24,2560]{2,1,0:T(8,128)(2,1)} reshape(bf16[4,24,64,40]{3,2,1,0:T(8,128)(2,1)S(1)} %copy.33) | data formatting | bytes 983040 | tf_op jit(solution)/shard_map/all_to_all | solution.py:65
  123.4 0.0 all-gather.2.cloned.1.call-update
  123.5 0.1 fusion.23
  123.6 0.1 fusion.35
  123.7 0.1 broadcast_in_dim.66
  123.9 0.0 collective-permute-done
  123.9 25.7 %all-reduce.5.cloned.1.call-done = f32[2,16,2176]{2,1,0:T(8,128)} async-done(((f32[2,16,2176]{2,1,0:T(8,128)}), f32[2,16,2176]{2,1,0:T(8,128)}) %all-reduce.5.cloned.1.call-update) | async-done | bytes 278544 | tf_op jit(solution)/shard_map/psum | solution.py:99
  149.5 1.2 fusion.31
  150.7 0.7 slice_bitcast_fusion
  151.4 8.4 %collective-permute-start.5 = (f32[16,2176]{1,0:T(8,128)S(1)}, f32[16,2176]{1,0:T(8,128)S(1)}, u32[]{:S(2)}, u32[]{:S(2)}) collective-permute-start(f32[16,2176]{1,0:T(8,128)S(1)} %get-tuple-element.11), channel_id=1, source_target_pairs={{1,0},{2,1},{3,2},{16,3},{17,16},{18,17},{19,18},{32,19},{33,32},{... | collective-permute-start | bytes 417800 | tf_op jit(solution)/shard_map/ppermute | solution.py:24
  159.8 1.9 collective-permute-start.4
  161.7 0.1 copy.39
  161.9 2.9 %collective-permute-done.5 = f32[16,2176]{1,0:T(8,128)S(1)} collective-permute-done((f32[16,2176]{1,0:T(8,128)S(1)}, f32[16,2176]{1,0:T(8,128)S(1)}, u32[]{:S(2)}, u32[]{:S(2)}) %collective-permute-start.5) | collective-permute-done | bytes 139296 | tf_op jit(solution)/shard_map/ppermute | solution.py:24
  164.8 5.0 %collective-permute-done.4 = f32[16,2176]{1,0:T(8,128)S(1)} collective-permute-done((f32[16,2176]{1,0:T(8,128)S(1)}, f32[16,2176]{1,0:T(8,128)S(1)}, u32[]{:S(2)}, u32[]{:S(2)}) %collective-permute-start.4) | collective-permute-done | bytes 139296 | tf_op jit(solution)/shard_map/ppermute | solution.py:22
  169.8 1.2 gather_fusion
  171.1 0.1 broadcast_in_dim.68
  171.2 0.8 select_select_fusion
  172.0 14.7 %all-gather.2.cloned.1.call-done = bf16[4,96,2560]{2,1,0:T(8,128)(2,1)} async-done(((bf16[4,24,2560]{2,1,0:T(8,128)(2,1)}), bf16[4,96,2560]{2,1,0:T(8,128)(2,1)}) %all-gather.2.cloned.1.call-update) | async-done | bytes 1966096 | tf_op jit(solution)/shard_map/all_gather | solution.py:74
  186.7 6.1 %fusion.44 = f32[4,96,384]{2,1,0:T(8,128)} fusion(bf16[4,96,2560]{2,1,0:T(8,128)(2,1)} %all-gather.2.cloned.1.call-done, bf16[4,2560,384]{2,1,0:T(8,128)(2,1)} %param.12), kind=kOutput, calls=%fused_computation.87 | convolution fusion | flops 754974720 | bytes 10420224 | tf_op jit(solution)/shard_map/srj,sjd->srd/dot_general | solution.py:72
  (34 shorter events, 0.4 us)
Async XLA Ops:
  7.2 4.5 %copy-start = (bf16[2,6]{1,0:T(2,128)(2,1)S(1)}, bf16[2,6]{1,0:T(2,128)(2,1)}, u32[]{:S(2)}) copy-start(bf16[2,6]{1,0:T(2,128)(2,1)} %param.13) | copy-start | bytes 76
  7.2 71.3 %all-reduce.3.cloned.1.call-start = ((), (), s32[]{:S(2)}) async-start(), calls=%async_computation.2 | async-start | bytes 3604480 | tf_op jit(solution)/shard_map/psum | solution.py:87
  11.7 3.8 %copy-start.1 = (bf16[2,6,40,5632]{3,2,1,0:T(8,128)(2,1)}, bf16[2,6,40,5632]{3,2,1,0:T(8,128)(2,1)S(1)}, u32[]{:S(2)}) copy-start(bf16[2,6,40,5632]{3,2,1,0:T(8,128)(2,1)S(1)} %broadcast_select_fusion) | copy-start | bytes 16220164
  11.7 3.8 %copy-start.7 = (s32[40]{0:T(128)S(1)}, s32[40]{0:T(128)}, u32[]{:S(2)}) copy-start(s32[40]{0:T(128)} %param.10) | copy-start | bytes 484
  11.7 3.8 %copy-start.8 = (s32[256]{0:T(256)S(1)}, s32[256]{0:T(256)}, u32[]{:S(2)}) copy-start(s32[256]{0:T(256)} %param.11) | copy-start | bytes 3076
  15.6 28.0 %slice-start = ((s8[5406720]{0:T(1024)(128)(4,1)}), s8[4194304]{0:T(1024)(128)(4,1)S(1)}, s32[]{:S(2)}) async-start(s8[5406720]{0:T(1024)(128)(4,1)} %bitcast.60), calls=%async_computation.4 | async-start | bytes 8388608
  40.6 3.0 %slice-start.1 = ((s8[5406720]{0:T(1024)(128)(4,1)}), s8[1212416]{0:T(1024)(128)(4,1)S(1)}, s32[]{:S(2)}) async-start(s8[5406720]{0:T(1024)(128)(4,1)} %bitcast.60), calls=%async_computation.5 | async-start | bytes 2424832
  49.3 17.8 %copy-start.5 = (s32[40,11]{0,1:T(8,128)S(1)}, s32[40,11]{0,1:T(8,128)}, u32[]{:S(2)}) copy-start(s32[40,11]{0,1:T(8,128)} %param.14) | copy-start | bytes 5284
  53.7 54.9 %copy-start.2 = (f32[16,2176]{1,0:T(8,128)S(1)}, f32[16,2176]{1,0:T(8,128)}, u32[]{:S(2)}) copy-start(f32[16,2176]{1,0:T(8,128)} %param.15) | copy-start | bytes 417796
  53.7 54.9 %copy-start.3 = (f32[16,2176]{1,0:T(8,128)S(1)}, f32[16,2176]{1,0:T(8,128)}, u32[]{:S(2)}) copy-start(f32[16,2176]{1,0:T(8,128)} %param.16) | copy-start | bytes 417796
  53.7 62.7 %all-to-all-start = ((bf16[64,2,1920]{2,1,0:T(2,128)(2,1)}), bf16[64,2,1920]{2,1,0:T(2,128)(2,1)S(1)}, u32[]{:S(2)}, u32[]{:S(2)}) async-start(bf16[64,2,1920]{2,1,0:T(2,128)(2,1)} %reshape.235), calls=%async_computation | async-start | bytes 983040 | tf_op jit(solution)/shard_map/all_to_all | solution.py:65
  67.1 82.5 %all-reduce.5.cloned.1.call-start = ((), (), s32[]{:S(2)}) async-start(), calls=%async_computation.3 | async-start | bytes 557056 | tf_op jit(solution)/shard_map/psum | solution.py:99
  83.2 16.4 %collective-permute-start.3 = (f32[272,256]{1,0:T(8,128)S(1)}, f32[272,256]{1,0:T(8,128)S(1)}, u32[]{:S(2)}, u32[]{:S(2)}) collective-permute-start(f32[272,256]{1,0:T(8,128)S(1)} %get-tuple-element.9), channel_id=1, source_target_pairs={{1,0},{2,1},{3,2},{16,3},{17,16},{18,17},{19,18},{32,19},{33,32},{... | collective-permute-start | bytes 835592 | tf_op jit(solution)/shard_map/ppermute | solution.py:24
  89.5 18.1 %collective-permute-start.2 = (f32[272,256]{1,0:T(8,128)S(1)}, f32[272,256]{1,0:T(8,128)S(1)}, u32[]{:S(2)}, u32[]{:S(2)}) collective-permute-start(f32[272,256]{1,0:T(8,128)S(1)} %get-tuple-element.8), channel_id=1, source_target_pairs={{0,1},{1,2},{2,3},{3,16},{16,17},{17,18},{18,19},{19,32},{32,33},{... | collective-permute-start | bytes 835592 | tf_op jit(solution)/shard_map/ppermute | solution.py:22
  107.6 15.8 %copy-start.6 = (s32[16,17]{1,0:T(8,128)S(1)}, s32[16,17]{1,0:T(8,128)}, u32[]{:S(2)}) copy-start(s32[16,17]{1,0:T(8,128)} %param.17) | copy-start | bytes 3268
  108.6 78.1 %all-gather.2.cloned.1.call-start = ((), (), s32[]{:S(2)}) async-start(), calls=%async_computation.1 | async-start | bytes 2457600 | tf_op jit(solution)/shard_map/all_gather | solution.py:74
  108.7 15.1 %collective-permute-start.1 = (f32[2,1,2176]{2,1,0:T(1,128)S(1)}, f32[2,1,2176]{2,1,0:T(1,128)S(1)}, u32[]{:S(2)}, u32[]{:S(2)}) collective-permute-start(f32[2,1,2176]{2,1,0:T(1,128)S(1)} %get-tuple-element.17), channel_id=1, source_target_pairs={{0,1},{1,2},{2,3},{3,16},{16,17},{17,18},{18,19},{19,32},{32,33},{... | collective-permute-start | bytes 52232 | tf_op jit(solution)/shard_map/ppermute | solution.py:22
  110.7 13.2 %collective-permute-start = (f32[2,1,2176]{2,1,0:T(1,128)S(1)}, f32[2,1,2176]{2,1,0:T(1,128)S(1)}, u32[]{:S(2)}, u32[]{:S(2)}) collective-permute-start(f32[2,1,2176]{2,1,0:T(1,128)S(1)} %get-tuple-element.16), channel_id=1, source_target_pairs={{1,0},{2,1},{3,2},{16,3},{17,16},{18,17},{19,18},{32,19},{33,32},{... | collective-permute-start | bytes 52232 | tf_op jit(solution)/shard_map/ppermute | solution.py:24
  151.4 41.4 %copy-start.4 = (f32[16,2176]{1,0:T(8,128)}, f32[16,2176]{1,0:T(8,128)S(1)}, u32[]{:S(2)}) copy-start(f32[16,2176]{1,0:T(8,128)S(1)} %get-tuple-element.11) | copy-start | bytes 417796
  151.4 13.4 %collective-permute-start.5 = (f32[16,2176]{1,0:T(8,128)S(1)}, f32[16,2176]{1,0:T(8,128)S(1)}, u32[]{:S(2)}, u32[]{:S(2)}) collective-permute-start(f32[16,2176]{1,0:T(8,128)S(1)} %get-tuple-element.11), channel_id=1, source_target_pairs={{1,0},{2,1},{3,2},{16,3},{17,16},{18,17},{19,18},{32,19},{33,32},{... | collective-permute-start | bytes 417800 | tf_op jit(solution)/shard_map/ppermute | solution.py:24
  159.8 10.0 %collective-permute-start.4 = (f32[16,2176]{1,0:T(8,128)S(1)}, f32[16,2176]{1,0:T(8,128)S(1)}, u32[]{:S(2)}, u32[]{:S(2)}) collective-permute-start(f32[16,2176]{1,0:T(8,128)S(1)} %get-tuple-element.11), channel_id=1, source_target_pairs={{0,1},{1,2},{2,3},{3,16},{16,17},{17,18},{18,19},{19,32},{32,33},{... | collective-permute-start | bytes 417800 | tf_op jit(solution)/shard_map/ppermute | solution.py:22
Sparse Core Ops, SparseCore 0:
  15.7 62.7 all-reduce.2
  108.7 40.7 all-reduce.4
  152.1 34.6 all-gather.1
where the time goes:
time: 200 us; the launch traced here: 199 us
  waiting for transfers between devices  75.1 us (38%)
  starting transfers between devices  39.7 us (20%)
  other arithmetic  37.9 us (19%)
  local copies, waits for them, and re-layouts  18.2 us (9%)
  matrix products  14.2 us (7%)
  between operations  14.2 us (7%)
    psum x1, waiting for transfers between devices, body(): tile_sums = lax.psum(arrived, 'lev')  25.7 us
    another operation x1, other arithmetic  25 us
    ppermute x3, starting transfers between devices, with_halo(): lax.ppermute(head, axis, [((i + 1) % count, i) for i in range(ends)])  20.5 us
    all_gather x1, waiting for transfers between devices, body(): lax.all_gather(regrouped, 'lev', axis=1, tiled=True)  14.7 us
    all_to_all x1, starting transfers between devices, body(): lax.all_to_all(coeffs.transpose(4, 1, 0, 3, 2).reshape(wave_count, lev_de...  13.3 us
    ppermute x3, waiting for transfers between devices, with_halo(): lax.ppermute(tail, axis, [(i, (i + 1) % count) for i in range(ends)])  13 us
    ppermute x3, waiting for transfers between devices, with_halo(): lax.ppermute(head, axis, [((i + 1) % count, i) for i in range(ends)])  11.1 us
    psum x1, waiting for transfers between devices, body(): totals = lax.psum(partial_sum, 'lev')  10.6 us
  transfers between devices with their start and end apart: 10, of which 7 were waited for; matrix products, arithmetic and copies ran while one was open for 26% of the time, Pallas kernels for 0%

commit v1 on v0

--- a/solution.py
+++ b/solution.py
@@ -84,7 +84,9 @@
         "ql,qljk->qjk", column_weight, masked, preferred_element_type=jnp.float32
     )
     quarter = lon_count // lax.axis_size("lev")
-    totals = lax.psum(partial_sum, "lev")
+    totals = partial_sum
+    for hop in (1, 2):
+        totals = totals + lax.ppermute(totals, "lev", [(dev, dev ^ hop) for dev in range(4)])
     own_flux = lax.dynamic_slice_in_dim(totals, lax.axis_index("lev") * quarter, quarter, 2)
     block_rows = (
         own_flux.reshape(FIELDS, lat_band, quarter // BLOCK, BLOCK)

time: 200 us -> 228 us (1.14)
  waiting for transfers between devices: 75.1 us -> 89 us
  starting transfers between devices: 39.7 us -> 50.6 us
  other arithmetic: 37.9 us -> 40.6 us
    ppermute x0 -> x2, waiting for transfers between devices: none -> 22 us  [body(): lax.ppermute(totals, 'lev', [(dev, dev ^ hop) for dev in range(4)])]
    psum x1 -> x0, waiting for transfers between devices: 10.6 us -> none  [body(): totals = lax.psum(partial_sum, 'lev')]
    all_gather x1, waiting for transfers between devices: 14.7 us -> 24.9 us  [body(): lax.all_gather(regrouped, 'lev', axis=1, tiled=True)]
    ppermute x3, waiting for transfers between devices: 11.1 us -> 4.6 us  [with_halo(): lax.ppermute(head, axis, [((i + 1) % count, i) for i in range(ends)])]
    ppermute x0 -> x2, starting transfers between devices: none -> 6.33 us  [body(): lax.ppermute(totals, 'lev', [(dev, dev ^ hop) for dev in range(4)])]
    ppermute x3, starting transfers between devices: 20.5 us -> 24.6 us  [with_halo(): lax.ppermute(head, axis, [((i + 1) % count, i) for i in range(ends)])]
    add x0 -> x2, other arithmetic: none -> 2.77 us  [body(): totals + lax.ppermute(totals, 'lev', [(dev, dev ^ hop) for dev in range(4)])]
    ppermute x3, waiting for transfers between devices: 13 us -> 10.5 us  [with_halo(): lax.ppermute(tail, axis, [(i, (i + 1) % count) for i in range(ends)])]
  transfers between devices with their start and end apart: 10 -> 11, of which waited for: 7 -> 7; matrix products, arithmetic and copies ran while one was open for 26% -> 25% of each run, Pallas kernels for 0% -> 0%
where the time goes in v1:
time: 228 us
  waiting for transfers between devices  89 us (39%)
  starting transfers between devices  50.6 us (22%)
  other arithmetic  40.6 us (18%)
  local copies, waits for them, and re-layouts  18.8 us (8%)
  between operations  14.5 us (6%)
  matrix products  14.2 us (6%)
    psum x1, waiting for transfers between devices, body(): tile_sums = lax.psum(arrived, 'lev')  27.1 us
    another operation x1, other arithmetic  25 us
    all_gather x1, waiting for transfers between devices, body(): lax.all_gather(regrouped, 'lev', axis=1, tiled=True)  24.9 us
    ppermute x3, starting transfers between devices, with_halo(): lax.ppermute(head, axis, [((i + 1) % count, i) for i in range(ends)])  24.6 us
    ppermute x2, waiting for transfers between devices, body(): lax.ppermute(totals, 'lev', [(dev, dev ^ hop) for dev in range(4)])  22 us
    all_to_all x1, starting transfers between devices, body(): lax.all_to_all(coeffs.transpose(4, 1, 0, 3, 2).reshape(wave_count, lev_de...  13.5 us
    ppermute x3, waiting for transfers between devices, with_halo(): lax.ppermute(tail, axis, [(i, (i + 1) % count) for i in range(ends)])  10.5 us
    ppermute x2, starting transfers between devices, body(): lax.ppermute(totals, 'lev', [(dev, dev ^ hop) for dev in range(4)])  6.33 us
  transfers between devices with their start and end apart: 11, of which 7 were waited for; matrix products, arithmetic and copies ran while one was open for 25% of the time, Pallas kernels for 0%

profile of v1, /device:TPU:1, one launch (start us, length us, event | category | flops | bytes accessed | tf_op | source)
XLA Modules:
  0.0 227.7 jit_solution(10624882624344308134)
XLA Ops:
  7.2 0.0 copy-start
  7.2 0.9 iota_compare_fusion
  8.0 3.6 %broadcast_select_fusion = bf16[2,6,40,5632]{3,2,1,0:T(8,128)(2,1)S(1)} fusion(bf16[2,6,40,5632]{3,2,1,0:T(8,128)(2,1)} %param.9, pred[40,5632]{1,0:T(8,128)(4,1)S(1)} %iota_compare_fusion), kind=kLoop, calls=%fused_computation.16 | loop fusion | flops 2703360 | bytes 11038720 | tf_op jit(solution)/shard_map/jit(_where)/select_n | solution.py:54
  11.7 0.0 copy-start.6
  11.7 0.0 copy-start.7
  11.7 2.4 %fusion = f32[2,1,40,5632]{3,1,2,0:T(1,128)S(1)} fusion(bf16[2,6,40,5632]{3,2,1,0:T(8,128)(2,1)S(1)} %broadcast_select_fusion, bf16[2,6,1,1]{1,0,2,3:T(2,128)(2,1)S(1)} %bitcast.61), kind=kOutput, calls=%fused_computation.3 | convolution fusion | flops 5406720 | bytes 7208984 | tf_op jit(solution)/shard_map/ql,qljk->qjk/dot_general | solution.py:83
  14.1 1.3 copy.61
  15.5 2.0 collective-permute-start.2
  17.5 0.1 compare_select_fusion
  17.6 25.0 %cosine_convert_fusion = (bf16[5632,256]{0,1:T(8,128)(2,1)S(1)}, bf16[5632,256]{0,1:T(8,128)(2,1)S(1)}) fusion(s32[256]{0:T(256)S(1)} %copy-done.7), kind=kLoop, calls=%fused_computation.9 | loop fusion | flops 17301504 | bytes 5768192 | tf_op jit(solution)/shard_map/convert
  42.6 2.9 %pad_maximum_fusion = bf16[5632,512]{0,1:T(8,128)(2,1)} fusion(bf16[5632,256]{0,1:T(8,128)(2,1)S(1)} %get-tuple-element.21, bf16[5632,256]{0,1:T(8,128)(2,1)S(1)} %get-tuple-element.20), kind=kLoop, calls=%fused_computation.7 | loop fusion | flops 11534336 | bytes 11534336 | tf_op jit(solution)/shard_map/concatenate | solution.py:35
  45.5 10.1 %collective-permute-done.2 = f32[2,40,5632]{2,1,0:T(8,128)} collective-permute-done((f32[2,40,5632]{2,1,0:T(8,128)}, f32[2,40,5632]{2,1,0:T(8,128)}, u32[]{:S(2)}, u32[]{:S(2)}) %collective-permute-start.2) | collective-permute-done | bytes 1802272 | tf_op jit(solution)/shard_map/ppermute | solution.py:89
  55.5 1.7 fusion.42
  57.2 4.3 %collective-permute-start.3 = (f32[2,40,5632]{2,1,0:T(8,128)S(1)}, f32[2,40,5632]{2,1,0:T(8,128)}, u32[]{:S(2)}, u32[]{:S(2)}) collective-permute-start(f32[2,40,5632]{2,1,0:T(8,128)S(1)} %fusion.42), channel_id=1, source_target_pairs={{0,8},{4,12},{8,0},{12,4},{1,9},{5,13},{9,1},{13,5},{2,10},{6,14},... | collective-permute-start | bytes 5406728 | tf_op jit(solution)/shard_map/ppermute | solution.py:89
  61.5 5.7 %fusion.15 = bf16[256,6,2,2,40]{0,4,3,1,2:T(8,128)(2,1)S(1)} fusion(bf16[2,256,5632,1,1]{2,1,0,4,3:T(8,128)(2,1)} %bitcast.63, bf16[2,6,40,5632]{3,2,1,0:T(8,128)(2,1)S(1)} %broadcast_select_fusion, f32[256,40]{0,1:T(8,128)S(1)} %compare_select_fusion), kind=kOutput, calls=%fused_computation.20 | convolution fusion | flops 2768732160 | bytes 11706368 | tf_op jit(solution)/shard_map/dot_general | solution.py:62
  67.2 0.0 copy-start.4
  67.2 0.8 copy.31
  68.0 1.8 copy.32
  69.8 3.4 %reshape.235 = bf16[64,2,1920]{2,1,0:T(2,128)(2,1)} reshape(bf16[256,24,40]{2,1,0:T(8,128)(2,1)S(1)} %copy.32) | data formatting | bytes 983040
  73.2 13.5 %all-to-all-start = ((bf16[64,2,1920]{2,1,0:T(2,128)(2,1)}), bf16[64,2,1920]{2,1,0:T(2,128)(2,1)S(1)}, u32[]{:S(2)}, u32[]{:S(2)}) async-start(bf16[64,2,1920]{2,1,0:T(2,128)(2,1)} %reshape.235), calls=%async_computation | async-start | bytes 983040 | tf_op jit(solution)/shard_map/all_to_all | solution.py:65
  86.7 0.0 all-reduce.2.cloned.1.call-start
  86.8 0.1 copy.35
  86.9 0.1 rem.47
  87.0 0.1 copy.36
  87.1 0.1 div.26
  87.3 0.1 copy.34
  87.4 0.1 ne.88
  87.5 11.9 %collective-permute-done.3 = f32[2,40,5632]{2,1,0:T(8,128)} collective-permute-done((f32[2,40,5632]{2,1,0:T(8,128)S(1)}, f32[2,40,5632]{2,1,0:T(8,128)}, u32[]{:S(2)}, u32[]{:S(2)}) %collective-permute-start.3) | collective-permute-done | bytes 1802272 | tf_op jit(solution)/shard_map/ppermute | solution.py:89
  99.4 1.1 dynamic-slice_add_fusion
  100.5 0.1 reshape.208
  100.6 0.3 copy.37
  101.0 3.1 %scatter_custom_fusion = f32[816,256]{1,0:T(8,128)S(1)} fusion(s32[440]{0:T(512)S(1)} %bitcast.80, f32[55,8,2,128]{3,2,1,0:T(2,128)S(1)} %bitcast.74, f32[]{:T(128)} %constant.40.clone.1), kind=kCustom, calls=%fused_computation.35 | custom fusion | flops 112640 | bytes 1286148 | tf_op jit(solution)/shard_map/scatter-add | solution.py:96
  104.2 10.5 %collective-permute-start.5 = (f32[272,256]{1,0:T(8,128)S(1)}, f32[272,256]{1,0:T(8,128)S(1)}, u32[]{:S(2)}, u32[]{:S(2)}) collective-permute-start(f32[272,256]{1,0:T(8,128)S(1)} %get-tuple-element.9), channel_id=1, source_target_pairs={{1,0},{2,1},{3,2},{16,3},{17,16},{18,17},{19,18},{32,19},{33,32},{... | collective-permute-start | bytes 835592 | tf_op jit(solution)/shard_map/ppermute | solution.py:24
  114.6 0.0 copy-start.1
  114.6 0.0 copy-start.2
  114.7 2.1 collective-permute-start.4
  116.7 4.3 %collective-permute-done.5 = f32[272,256]{1,0:T(8,128)S(1)} collective-permute-done((f32[272,256]{1,0:T(8,128)S(1)}, f32[272,256]{1,0:T(8,128)S(1)}, u32[]{:S(2)}, u32[]{:S(2)}) %collective-permute-start.5) | collective-permute-done | bytes 278560 | tf_op jit(solution)/shard_map/ppermute | solution.py:24
  121.0 10.5 %collective-permute-done.4 = f32[272,256]{1,0:T(8,128)S(1)} collective-permute-done((f32[272,256]{1,0:T(8,128)S(1)}, f32[272,256]{1,0:T(8,128)S(1)}, u32[]{:S(2)}, u32[]{:S(2)}) %collective-permute-start.4) | collective-permute-done | bytes 278560 | tf_op jit(solution)/shard_map/ppermute | solution.py:22
  131.4 0.1 fusion.24
  131.5 0.1 reshape.210
  131.7 0.8 reshape.211
  132.5 0.0 all-reduce.2.cloned.1.call-update
  132.5 0.3 all-gather.2.cloned.1.call-start
  132.8 2.5 %reshape.236 = bf16[256,24,40]{2,1,0:T(8,128)(2,1)S(1)} reshape(bf16[64,2,1920]{2,1,0:T(2,128)(2,1)S(1)} %all-to-all-done) | data formatting | bytes 983040
  135.3 0.6 copy.33
  135.9 3.9 %all_to_all.16 = bf16[4,24,2560]{2,1,0:T(8,128)(2,1)} reshape(bf16[4,24,64,40]{3,2,1,0:T(8,128)(2,1)S(1)} %copy.33) | data formatting | bytes 983040 | tf_op jit(solution)/shard_map/all_to_all | solution.py:65
  139.8 0.0 all-gather.2.cloned.1.call-update
  139.8 1.9 collective-permute-start.1
  141.8 5.8 %collective-permute-start = (f32[2,1,2176]{2,1,0:T(1,128)S(1)}, f32[2,1,2176]{2,1,0:T(1,128)S(1)}, u32[]{:S(2)}, u32[]{:S(2)}) collective-permute-start(f32[2,1,2176]{2,1,0:T(1,128)S(1)} %get-tuple-element.16), channel_id=1, source_target_pairs={{1,0},{2,1},{3,2},{16,3},{17,16},{18,17},{19,18},{32,19},{33,32},{... | collective-permute-start | bytes 52232 | tf_op jit(solution)/shard_map/ppermute | solution.py:24
  147.5 0.1 fusion.35
  147.6 0.1 fusion.23
  147.8 0.1 broadcast_in_dim.66
  147.9 0.1 copy.39
  148.0 0.3 collective-permute-done
  148.4 27.1 %all-reduce.2.cloned.1.call-done = f32[2,16,2176]{2,1,0:T(8,128)} async-done(((f32[2,16,2176]{2,1,0:T(8,128)}), f32[2,16,2176]{2,1,0:T(8,128)}) %all-reduce.2.cloned.1.call-update) | async-done | bytes 278544 | tf_op jit(solution)/shard_map/psum | solution.py:101
  175.5 1.2 fusion.31
  176.7 0.7 slice_bitcast_fusion
  177.3 8.4 %collective-permute-start.7 = (f32[16,2176]{1,0:T(8,128)S(1)}, f32[16,2176]{1,0:T(8,128)S(1)}, u32[]{:S(2)}, u32[]{:S(2)}) collective-permute-start(f32[16,2176]{1,0:T(8,128)S(1)} %get-tuple-element.11), channel_id=1, source_target_pairs={{1,0},{2,1},{3,2},{16,3},{17,16},{18,17},{19,18},{32,19},{33,32},{... | collective-permute-start | bytes 417800 | tf_op jit(solution)/shard_map/ppermute | solution.py:24
  185.8 1.9 collective-permute-start.6
  187.7 24.9 %all-gather.2.cloned.1.call-done = bf16[4,96,2560]{2,1,0:T(8,128)(2,1)} async-done(((bf16[4,24,2560]{2,1,0:T(8,128)(2,1)}), bf16[4,96,2560]{2,1,0:T(8,128)(2,1)}) %all-gather.2.cloned.1.call-update) | async-done | bytes 1966096 | tf_op jit(solution)/shard_map/all_gather | solution.py:74
  212.6 6.1 %fusion.45 = f32[4,96,384]{2,1,0:T(8,128)} fusion(bf16[4,96,2560]{2,1,0:T(8,128)(2,1)} %all-gather.2.cloned.1.call-done, bf16[4,2560,384]{2,1,0:T(8,128)(2,1)} %param.12), kind=kOutput, calls=%fused_computation.88 | convolution fusion | flops 754974720 | bytes 10420224 | tf_op jit(solution)/shard_map/srj,sjd->srd/dot_general | solution.py:72
  218.7 1.2 gather_fusion
  219.9 0.1 broadcast_in_dim.68
  220.1 0.8 select_select_fusion
  (29 shorter events, 0.3 us)
Async XLA Ops:
  7.2 4.5 %copy-start = (bf16[2,6]{1,0:T(2,128)(2,1)S(1)}, bf16[2,6]{1,0:T(2,128)(2,1)}, u32[]{:S(2)}) copy-start(bf16[2,6]{1,0:T(2,128)(2,1)} %param.13) | copy-start | bytes 76
  11.7 5.8 %copy-start.6 = (s32[40]{0:T(128)S(1)}, s32[40]{0:T(128)}, u32[]{:S(2)}) copy-start(s32[40]{0:T(128)} %param.10) | copy-start | bytes 484
  11.7 5.8 %copy-start.7 = (s32[256]{0:T(256)S(1)}, s32[256]{0:T(256)}, u32[]{:S(2)}) copy-start(s32[256]{0:T(256)} %param.11) | copy-start | bytes 3076
  15.5 40.0 %collective-permute-start.2 = (f32[2,40,5632]{2,1,0:T(8,128)}, f32[2,40,5632]{2,1,0:T(8,128)}, u32[]{:S(2)}, u32[]{:S(2)}) collective-permute-start(f32[2,40,5632]{2,1,0:T(8,128)} %bitcast.59), channel_id=1, source_target_pairs={{0,4},{4,0},{8,12},{12,8},{1,5},{5,1},{9,13},{13,9},{2,6},{6,2},{1... | collective-permute-start | bytes 5406728 | tf_op jit(solution)/shard_map/ppermute | solution.py:89
  57.2 42.2 %collective-permute-start.3 = (f32[2,40,5632]{2,1,0:T(8,128)S(1)}, f32[2,40,5632]{2,1,0:T(8,128)}, u32[]{:S(2)}, u32[]{:S(2)}) collective-permute-start(f32[2,40,5632]{2,1,0:T(8,128)S(1)} %fusion.42), channel_id=1, source_target_pairs={{0,8},{4,12},{8,0},{12,4},{1,9},{5,13},{9,1},{13,5},{2,10},{6,14},... | collective-permute-start | bytes 5406728 | tf_op jit(solution)/shard_map/ppermute | solution.py:89
  67.2 19.6 %copy-start.4 = (s32[40,11]{0,1:T(8,128)S(1)}, s32[40,11]{0,1:T(8,128)}, u32[]{:S(2)}) copy-start(s32[40,11]{0,1:T(8,128)} %param.14) | copy-start | bytes 5284
  73.2 59.5 %all-to-all-start = ((bf16[64,2,1920]{2,1,0:T(2,128)(2,1)}), bf16[64,2,1920]{2,1,0:T(2,128)(2,1)S(1)}, u32[]{:S(2)}, u32[]{:S(2)}) async-start(bf16[64,2,1920]{2,1,0:T(2,128)(2,1)} %reshape.235), calls=%async_computation | async-start | bytes 983040 | tf_op jit(solution)/shard_map/all_to_all | solution.py:65
  86.7 88.8 %all-reduce.2.cloned.1.call-start = ((), (), s32[]{:S(2)}) async-start(), calls=%async_computation.2 | async-start | bytes 557056 | tf_op jit(solution)/shard_map/psum | solution.py:101
  104.2 16.8 %collective-permute-start.5 = (f32[272,256]{1,0:T(8,128)S(1)}, f32[272,256]{1,0:T(8,128)S(1)}, u32[]{:S(2)}, u32[]{:S(2)}) collective-permute-start(f32[272,256]{1,0:T(8,128)S(1)} %get-tuple-element.9), channel_id=1, source_target_pairs={{1,0},{2,1},{3,2},{16,3},{17,16},{18,17},{19,18},{32,19},{33,32},{... | collective-permute-start | bytes 835592 | tf_op jit(solution)/shard_map/ppermute | solution.py:24
  114.6 25.2 %copy-start.1 = (f32[16,2176]{1,0:T(8,128)S(1)}, f32[16,2176]{1,0:T(8,128)}, u32[]{:S(2)}) copy-start(f32[16,2176]{1,0:T(8,128)} %param.15) | copy-start | bytes 417796
  114.6 25.2 %copy-start.2 = (f32[16,2176]{1,0:T(8,128)S(1)}, f32[16,2176]{1,0:T(8,128)}, u32[]{:S(2)}) copy-start(f32[16,2176]{1,0:T(8,128)} %param.16) | copy-start | bytes 417796
  114.7 16.8 %collective-permute-start.4 = (f32[272,256]{1,0:T(8,128)S(1)}, f32[272,256]{1,0:T(8,128)S(1)}, u32[]{:S(2)}, u32[]{:S(2)}) collective-permute-start(f32[272,256]{1,0:T(8,128)S(1)} %get-tuple-element.8), channel_id=1, source_target_pairs={{0,1},{1,2},{2,3},{3,16},{16,17},{17,18},{18,19},{19,32},{32,33},{... | collective-permute-start | bytes 835592 | tf_op jit(solution)/shard_map/ppermute | solution.py:22
  131.5 16.1 %copy-start.5 = (s32[16,17]{1,0:T(8,128)S(1)}, s32[16,17]{1,0:T(8,128)}, u32[]{:S(2)}) copy-start(s32[16,17]{1,0:T(8,128)} %param.17) | copy-start | bytes 3268
  132.5 80.1 %all-gather.2.cloned.1.call-start = ((), (), s32[]{:S(2)}) async-start(), calls=%async_computation.1 | async-start | bytes 2457600 | tf_op jit(solution)/shard_map/all_gather | solution.py:74
  139.8 8.2 %collective-permute-start.1 = (f32[2,1,2176]{2,1,0:T(1,128)S(1)}, f32[2,1,2176]{2,1,0:T(1,128)S(1)}, u32[]{:S(2)}, u32[]{:S(2)}) collective-permute-start(f32[2,1,2176]{2,1,0:T(1,128)S(1)} %get-tuple-element.17), channel_id=1, source_target_pairs={{0,1},{1,2},{2,3},{3,16},{16,17},{17,18},{18,19},{19,32},{32,33},{... | collective-permute-start | bytes 52232 | tf_op jit(solution)/shard_map/ppermute | solution.py:22
  141.8 6.6 %collective-permute-start = (f32[2,1,2176]{2,1,0:T(1,128)S(1)}, f32[2,1,2176]{2,1,0:T(1,128)S(1)}, u32[]{:S(2)}, u32[]{:S(2)}) collective-permute-start(f32[2,1,2176]{2,1,0:T(1,128)S(1)} %get-tuple-element.16), channel_id=1, source_target_pairs={{1,0},{2,1},{3,2},{16,3},{17,16},{18,17},{19,18},{32,19},{33,32},{... | collective-permute-start | bytes 52232 | tf_op jit(solution)/shard_map/ppermute | solution.py:24
  177.3 41.3 %copy-start.3 = (f32[16,2176]{1,0:T(8,128)}, f32[16,2176]{1,0:T(8,128)S(1)}, u32[]{:S(2)}) copy-start(f32[16,2176]{1,0:T(8,128)S(1)} %get-tuple-element.11) | copy-start | bytes 417796
  177.3 41.3 %collective-permute-start.7 = (f32[16,2176]{1,0:T(8,128)S(1)}, f32[16,2176]{1,0:T(8,128)S(1)}, u32[]{:S(2)}, u32[]{:S(2)}) collective-permute-start(f32[16,2176]{1,0:T(8,128)S(1)} %get-tuple-element.11), channel_id=1, source_target_pairs={{1,0},{2,1},{3,2},{16,3},{17,16},{18,17},{19,18},{32,19},{33,32},{... | collective-permute-start | bytes 417800 | tf_op jit(solution)/shard_map/ppermute | solution.py:24
  185.8 32.8 %collective-permute-start.6 = (f32[16,2176]{1,0:T(8,128)S(1)}, f32[16,2176]{1,0:T(8,128)S(1)}, u32[]{:S(2)}, u32[]{:S(2)}) collective-permute-start(f32[16,2176]{1,0:T(8,128)S(1)} %get-tuple-element.11), channel_id=1, source_target_pairs={{0,1},{1,2},{2,3},{3,16},{16,17},{17,18},{18,19},{19,32},{32,33},{... | collective-permute-start | bytes 417800 | tf_op jit(solution)/shard_map/ppermute | solution.py:22
Sparse Core Ops, SparseCore 0:
  132.6 42.8 all-reduce.1
  177.9 34.6 all-gather.1
